TPU v7x, 32 devices: a whole 2x2x4 slice. The times are simulated.
32 devices in a mesh: groups: 2 (over y), replica: 8 (over z, x), tensor: 2 (over core).
Axes of the slice: x: 2, y: 2, z: 4, core: 2. Of those that a mesh axis runs over, the one named last changes fastest.
Arguments:
- hidden: bfloat16 [4, 1024, 4096], P(None, ('groups', 'replica'), 'tensor'), parts along dimension 1, may hold values from -6 to 6
- query_key_value_weight: bfloat16 [4096, 384], P('tensor'), may hold values from -0.09375 to 0.09375
- adapter_down_weight: bfloat16 [16, 4096, 32], P('replica', 'tensor'), may hold values from -0.09375 to 0.09375
- adapter_up_weight: bfloat16 [16, 16, 256], P('replica'), may hold values from -1.5 to 1.5
- key_value_pool: bfloat16 [16, 192, 16, 256], P(('groups', 'replica'), None, 'tensor'), parts along dimension 0, may hold values from -255 to 255
- adapter_replica: int32 [1024, 1], P(('groups', 'replica')), parts along dimension 0, may hold values from 0 to 7; in each aligned block of 64 rows (0 to 63, 64 to 127, ...) at most 16 rows name the same one
- adapter_choice_index: int32 [1024], P(('groups', 'replica')), parts along dimension 0, may hold values from 0 to 1
- cached_length: int32 [16, 64], P(('groups', 'replica')), parts along dimension 0, may hold values from 1 to 48, 1536 in all within a row
- request_block_table: int32 [16, 192], P(('groups', 'replica')), parts along dimension 0, may hold values from 0 to 191, each once within a row
Outputs:
- attn_out: bfloat16 [4, 1024, 128], P(None, ('groups', 'replica')), parts along dimension 1
There are 2 independent parts, one for each index of `groups`. A program takes and returns all parts, laid end to end along the dimension named above; an argument that names none is the same for every part. Nothing has to cross between parts.
Inputs may be any that keep to these rules, and one draw needn't show every extreme that they name: `adapter_replica`: in the rows of one replica no replica is named more than 16 times, a bound that some block reaches. `cached_length`: each row sums to 1536; request j of a replica owns entries j * 3 to j * 3 + 2 of its row of request_block_table. `request_block_table`: each row is a permutation of the replica's 192 blocks.
All inputs are finite; a program needn't handle non-finite values.
Results may differ from a plain program's by a relative error of at most 0.007.
Values may be sent and summed in bfloat16 or wider, within the bound.
A program may use at most 64 MiB of HBM per device.

v0:
```python
import math

import jax
import jax.numpy as jnp
from jax import lax
from jax.sharding import PartitionSpec as P

rope_base = 500000.0
neg_fill = -1e30


def combined_all(part, axis, combine):
    gathered = jax.tree.map(lambda a: lax.all_gather(a, axis), part)

    def take(source):
        return jax.tree.map(lambda a: lax.dynamic_index_in_dim(a, source, 0, False), gathered)

    return lax.fori_loop(
        1, lax.axis_size(axis), lambda source, state: combine(state, take(source)), take(0)
    )


def rotate(vector, position):
    half_len = vector.shape[-1] // 2
    frequency = rope_base ** (-(jnp.arange(half_len, dtype=jnp.float32) * 2.0) / vector.shape[-1])
    angles = position[..., None].astype(jnp.float32) * frequency
    cosine = jnp.cos(angles)
    sine_part = jnp.sin(angles)
    first_part = vector[..., :half_len]
    second = vector[..., half_len:]
    return jnp.concatenate(
        [first_part * cosine - second * sine_part, second * cosine + first_part * sine_part],
        axis=-1,
    )


def adapter_delta(row_payload, choice_index, adapter_down_weight, adapter_up_weight):
    req_count, step_count, feat_width = row_payload.shape
    adapter_rank_width = adapter_up_weight.shape[1]
    head_width = adapter_up_weight.shape[2] // 2
    flattened_rows = row_payload.reshape(req_count * step_count, feat_width)
    summed = jnp.zeros((req_count, step_count, 2 * head_width), jnp.float32)
    highest_precision = lax.Precision.HIGHEST
    for adapter_slot in range(adapter_down_weight.shape[0]):
        reduced_rank = jnp.dot(
            flattened_rows, adapter_down_weight[adapter_slot], preferred_element_type=jnp.float32
        ).reshape(req_count, step_count, 2 * adapter_rank_width)
        up_matrix = adapter_up_weight[adapter_slot].astype(jnp.float32)
        query_term = jnp.einsum(
            "nsr,re->nse",
            reduced_rank[..., :adapter_rank_width],
            up_matrix[:, :head_width],
            precision=highest_precision,
        )
        value_term = jnp.einsum(
            "nsr,re->nse",
            reduced_rank[..., adapter_rank_width:],
            up_matrix[:, head_width:],
            precision=highest_precision,
        )
        chosen = (choice_index == adapter_slot)[:, None, None]
        summed = summed + jnp.where(chosen, jnp.concatenate([query_term, value_term], axis=-1), 0.0)
    return summed


def project_input(row_payload, query_key_value_weight, adapter_term):
    req_count, step_count, feat_width = row_payload.shape
    base_part = jnp.dot(
        row_payload.reshape(req_count * step_count, feat_width),
        query_key_value_weight,
        preferred_element_type=jnp.float32,
    ).reshape(req_count, step_count, -1)
    head_width = adapter_term.shape[-1] // 2
    middle_zeros = jnp.zeros(adapter_term.shape[:-1] + (head_width,), jnp.float32)
    return base_part + jnp.concatenate(
        [adapter_term[..., :head_width], middle_zeros, adapter_term[..., head_width:]], axis=-1
    )


def attend(summed, seq_lens, cached, cache_pos, keep_new):
    head_width = cached.shape[-1] // 2
    step_count = summed.shape[1]
    step_ids = jnp.arange(step_count, dtype=jnp.int32)
    position = seq_lens[:, None] + step_ids[None, :]
    queries = rotate(summed[..., :head_width], position).astype(jnp.bfloat16)
    fresh_k = rotate(summed[..., head_width : 2 * head_width], position).astype(jnp.bfloat16)
    fresh_v = summed[..., 2 * head_width :].astype(jnp.bfloat16)
    scaling = 1.0 / math.sqrt(head_width)
    old_scores = (
        jnp.einsum(
            "nsh,nph->nsp", queries, cached[..., :head_width], preferred_element_type=jnp.float32
        )
        * scaling
    )
    new_scores = (
        jnp.einsum("nsh,nth->nst", queries, fresh_k, preferred_element_type=jnp.float32) * scaling
    )
    old_mask = jnp.broadcast_to(
        cache_pos[None, None, :] < seq_lens[:, None, None], old_scores.shape
    )
    new_mask = jnp.broadcast_to(
        (step_ids[None, :, None] >= step_ids[None, None, :]) & keep_new, new_scores.shape
    )
    old_scores = jnp.where(old_mask, old_scores, neg_fill)
    new_scores = jnp.where(new_mask, new_scores, neg_fill)
    peak_val = jnp.maximum(jnp.max(old_scores, axis=-1), jnp.max(new_scores, axis=-1))
    old_exp = jnp.where(old_mask, jnp.exp(old_scores - peak_val[..., None]), 0.0)
    new_exp = jnp.where(new_mask, jnp.exp(new_scores - peak_val[..., None]), 0.0)
    total_sum = jnp.sum(old_exp, axis=-1) + jnp.sum(new_exp, axis=-1)
    accum = jnp.einsum(
        "nsp,nph->nsh",
        old_exp.astype(jnp.bfloat16),
        cached[..., head_width:],
        preferred_element_type=jnp.float32,
    )
    accum = accum + jnp.einsum(
        "nst,nth->nsh", new_exp.astype(jnp.bfloat16), fresh_v, preferred_element_type=jnp.float32
    )
    return (peak_val, total_sum, accum)


def combine(first_part, second):
    peak_val = jnp.maximum(first_part[0], second[0])
    left_scale = jnp.exp(first_part[0] - peak_val)
    right_scale = jnp.exp(second[0] - peak_val)
    return (
        peak_val,
        first_part[1] * left_scale + second[1] * right_scale,
        first_part[2] * left_scale[..., None] + second[2] * right_scale[..., None],
    )


def serve_rows(value_partial, seq_lens, cached, cache_pos, keep_new):
    summed = lax.psum(value_partial, "tensor")
    stats = attend(summed, seq_lens, cached, cache_pos, keep_new)
    peak_val, total_sum, accum = combined_all(stats, "tensor", combine)
    return (accum / total_sum[..., None]).astype(jnp.bfloat16)


def on_device(
    hidden,
    query_key_value_weight,
    adapter_down_weight,
    adapter_up_weight,
    key_value_pool,
    adapter_replica,
    adapter_choice_index,
    cached_length,
    request_block_table,
):
    step_count, req_count, feat_width = hidden.shape
    half_len = key_value_pool.shape[2]
    head_width = key_value_pool.shape[3] // 2
    blocks = request_block_table.shape[1] // req_count
    replica_count = lax.axis_size("replica")
    slot_cap = max(2, (2 * req_count + replica_count - 1) // replica_count)
    tensor_id = lax.axis_index("tensor")
    keep_new = tensor_id == 0
    cache_pos = (
        jnp.arange(blocks, dtype=jnp.int32)[:, None] * (half_len * lax.axis_size("tensor"))
        + tensor_id * half_len
        + jnp.arange(half_len, dtype=jnp.int32)[None, :]
    ).reshape(-1)
    seq_lens = cached_length[0]
    home_rep = adapter_replica[:, 0]
    order_idx = jnp.arange(req_count, dtype=jnp.int32)
    earlier = (home_rep[:, None] == home_rep[None, :]) & (order_idx[None, :] < order_idx[:, None])
    slot_of = home_rep * slot_cap + jnp.sum(earlier.astype(jnp.int32), axis=1)
    slot_total = replica_count * slot_cap
    local_rows = jnp.swapaxes(hidden, 0, 1)
    row_buffer = (
        jnp.zeros((slot_total, step_count, feat_width), hidden.dtype).at[slot_of].set(local_rows)
    )
    cached = key_value_pool[0][request_block_table[0].reshape(req_count, blocks)].reshape(
        req_count, blocks * half_len, 2 * head_width
    )
    cache_buffer = (
        jnp.zeros((slot_total, blocks * half_len, 2 * head_width), key_value_pool.dtype)
        .at[slot_of]
        .set(cached)
    )
    meta_ints = (
        jnp.zeros((slot_total, 2), jnp.int32)
        .at[slot_of]
        .set(jnp.stack([adapter_choice_index, seq_lens], axis=1))
    )
    landed_rows, arrived_cache, landed_integers = (
        lax.all_to_all(row_buffer, "replica", split_axis=0, concat_axis=0, tiled=True),
        lax.all_to_all(cache_buffer, "replica", split_axis=0, concat_axis=0, tiled=True),
        lax.all_to_all(meta_ints, "replica", split_axis=0, concat_axis=0, tiled=True),
    )
    adapter_term = adapter_delta(
        landed_rows, landed_integers[:, 0], adapter_down_weight, adapter_up_weight
    )
    value_partial = project_input(landed_rows, query_key_value_weight, adapter_term)
    result = serve_rows(value_partial, landed_integers[:, 1], arrived_cache, cache_pos, keep_new)
    returned = lax.all_to_all(result, "replica", split_axis=0, concat_axis=0, tiled=True)
    return jnp.swapaxes(returned[slot_of], 0, 1)


def solution(mesh):
    placed = (
        P(None, ("groups", "replica"), "tensor"),
        P("tensor", None),
        P("replica", "tensor", None),
        P("replica", None, None),
        P(("groups", "replica"), None, "tensor", None),
        P(("groups", "replica"), None),
        P(("groups", "replica")),
        P(("groups", "replica"), None),
        P(("groups", "replica"), None),
    )
    return jax.shard_map(
        on_device,
        mesh=mesh,
        in_specs=placed,
        out_specs=P(None, ("groups", "replica"), None),
        check_vma=False,
    )
```

profile of v0, /device:TPU:1, one launch (start us, length us, event | category | flops | bytes accessed | tf_op | source)
XLA Modules:
  0.0 162.4 jit_solution(6932539938945060157)
XLA Ops:
  6.5 1.0 convert_reduce_fusion
  7.5 0.7 fusion.69
  8.2 0.7 pad_add_fusion
  9.0 0.8 scatter_custom_fusion
  9.7 0.7 copy.109
  10.4 6.4 %all-to-all-start = ((s32[8,16,2]{1,2,0:T(2,128)}), s32[8,16,2]{1,2,0:T(2,128)S(1)}, u32[]{:S(2)}, u32[]{:S(2)}) async-start(s32[8,16,2]{1,2,0:T(2,128)} %copy.109), calls=%async_computation | async-start | bytes 16384 | tf_op jit(solution)/shard_map/all_to_all | solution.py:190
  16.8 2.0 %copy.111 = bf16[64,4,2048]{2,1,0:T(4,128)(2,1)S(1)} copy(bf16[64,4,2048]{2,0,1:T(8,128)(2,1)} %bitcast.55) | data formatting | bytes 2097152 | tf_op jit(solution)/shard_map/transpose | solution.py:170
  18.8 2.4 %broadcast_in_dim.81 = bf16[128,4,2048]{2,1,0:T(4,128)(2,1)} broadcast(bf16[]{:T(256)} %constant.24.clone.1), dimensions={} | broadcast | bytes 2097154 | tf_op jit(solution)/shard_map/broadcast_in_dim | solution.py:172
  21.2 8.1 %scatter_fusion = bf16[128,4,2048]{2,1,0:T(4,128)(2,1)} fusion(bf16[128,4,2048]{2,1,0:T(4,128)(2,1)} %broadcast_in_dim.81, s32[64]{0:T(128)S(1)} %fusion.69, bf16[64,4,2048]{2,1,0:T(4,128)(2,1)S(1)} %copy.111), kind=kCustom, calls=%fused_computation.3 | custom fusion | bytes 3145984 | tf_op jit(solution)/shard_map/scatter | solution.py:172
  29.3 5.6 %all-to-all-start.1 = ((bf16[128,4,2048]{2,1,0:T(4,128)(2,1)}), bf16[128,4,2048]{2,1,0:T(4,128)(2,1)}, u32[]{:S(2)}, u32[]{:S(2)}) async-start(bf16[128,4,2048]{2,1,0:T(4,128)(2,1)} %scatter_fusion), calls=%async_computation.1 | async-start | bytes 4194304 | tf_op jit(solution)/shard_map/all_to_all | solution.py:188
  34.9 0.5 broadcast.145
  35.4 0.7 reduce.3
  36.4 0.8 gather_fusion
  37.2 1.3 broadcast_in_dim.86
  38.5 8.1 %scatter_fusion.1 = bf16[128,24,256]{2,1,0:T(8,128)(2,1)} fusion(bf16[128,24,256]{2,1,0:T(8,128)(2,1)} %broadcast_in_dim.86, s32[64]{0:T(128)S(1)} %fusion.69, bf16[64,24,256]{2,1,0:T(8,128)(2,1)S(1)} %bitcast.54), kind=kCustom, calls=%fused_computation.4 | custom fusion | bytes 2359552 | tf_op jit(solution)/shard_map/scatter | solution.py:180
  46.8 35.0 %all-to-all-done.1 = bf16[128,4,2048]{2,1,0:T(4,128)(2,1)} async-done(((bf16[128,4,2048]{2,1,0:T(4,128)(2,1)}), bf16[128,4,2048]{2,1,0:T(4,128)(2,1)}, u32[]{:S(2)}, u32[]{:S(2)}) %all-to-all-start.1) | async-done | bytes 2097184 | tf_op jit(solution)/shard_map/all_to_all | solution.py:188
  81.8 5.3 %all-to-all-start.2 = ((bf16[128,24,256]{2,1,0:T(8,128)(2,1)}), bf16[128,24,256]{2,1,0:T(8,128)(2,1)S(1)}, u32[]{:S(2)}, u32[]{:S(2)}) async-start(bf16[128,24,256]{2,1,0:T(8,128)(2,1)} %scatter_fusion.1), calls=%async_computation.2 | async-start | bytes 3145728 | tf_op jit(solution)/shard_map/all_to_all | solution.py:189
  87.1 0.2 all-reduce.2.cloned.1.call-start
  87.3 3.9 %fusion = f32[128,4,32]{0,2,1:T(8,128)S(1)} fusion(bf16[128,4,2048]{2,1,0:T(4,128)(2,1)} %all-to-all-done.1, bf16[2,2048,32]{1,2,0:T(8,128)(2,1)S(1)} %copy-done.12), kind=kOutput, calls=%fused_computation.5 | convolution fusion | flops 67108864 | bytes 2293760 | tf_op jit(solution)/shard_map/dot_general | solution.py:45
  91.2 0.4 fusion.51
  91.6 0.4 fusion.53
  92.0 3.9 %fusion.2 = f32[128,4,32]{0,2,1:T(8,128)S(1)} fusion(bf16[128,4,2048]{2,1,0:T(4,128)(2,1)} %all-to-all-done.1, bf16[2,2048,32]{1,2,0:T(8,128)(2,1)S(1)} %copy-done.12), kind=kOutput, calls=%fused_computation.7 | convolution fusion | flops 67108864 | bytes 2293760 | tf_op jit(solution)/shard_map/dot_general | solution.py:45
  95.9 0.4 fusion.55
  96.3 0.4 fusion.57
  96.9 5.1 %fusion.7 = f32[128,4,384]{2,0,1:T(8,128)} fusion(bf16[2048,384]{1,0:T(8,128)(2,1)S(1)} %copy-done, bf16[128,4,2048]{2,1,0:T(4,128)(2,1)} %all-to-all-done.1, f32[128,4,128]{2,0,1:T(8,128)S(1)} %get-tuple-element.37, f32[128,4,128]{2,0,1:T(8,128)S(1)} %get-tuple-element.36, f32[384]{0:T(512)S(1)} %pad.5.clone), kind=kOutput, calls=%fused_computation.12 | convolution fusion | flops 805896192 | bytes 4982272 | tf_op jit(solution)/shard_map/dot_general | solution.py:68
  102.2 0.7 broadcast_compare_fusion
  102.8 20.3 %all-reduce.2.cloned.1.call-done = f32[128,4,384]{2,0,1:T(8,128)} async-done(((f32[128,4,384]{2,0,1:T(8,128)}), f32[128,4,384]{2,0,1:T(8,128)}) %all-reduce.2.cloned.1.call-update) | async-done | bytes 786448 | tf_op jit(solution)/shard_map/psum | solution.py:134
  123.1 2.4 %fusion.30 = (bf16[128,4,64]{2,0,1:T(8,128)(2,1)S(1)}, bf16[128,4,64]{2,0,1:T(8,128)(2,1)S(1)}, bf16[128,4,64]{2,0,1:T(8,128)(2,1)S(1)}, bf16[128,4,64]{2,0,1:T(8,128)(2,1)S(1)}) fusion(f32[128,4,384]{2,0,1:T(8,128)} %all-reduce.2.cloned.1.call-done, f32[64]{0:T(128)S(1)} %multiply_power_fusion, f32[128,4]{0,1:T(4,128)S(1)} %add_convert_fusion), kind=kLoop, calls=%fused_computation.37 | loop fusion | flops 557056 | bytes 788736 | tf_op jit(solution)/shard_map/convert.1
  125.7 0.6 copy-done.6
  126.4 0.3 fusion.42
  126.8 1.5 fusion.74
  128.6 0.8 fusion.63
  129.4 1.8 %all-gather.1 = f32[256,4]{0,1:T(4,128)S(1)} all-gather(f32[128,4]{0,1:T(4,128)S(1)} %max.31), channel_id=3, replica_groups=mesh['groups'=2,'replica'=8,'tensor'=2] {'tensor'}, dimensions={0}, use_global_device_ids=true | all-gather | bytes 6144 | tf_op jit(solution)/shard_map/all_gather | solution.py:13
  131.1 1.1 fusion.36
  132.3 1.8 %all-gather.2 = f32[256,4]{0,1:T(4,128)S(1)} all-gather(f32[128,4]{0,1:T(4,128)S(1)} %add.146), channel_id=4, replica_groups=mesh['groups'=2,'replica'=8,'tensor'=2] {'tensor'}, dimensions={0}, use_global_device_ids=true | all-gather | bytes 6144 | tf_op jit(solution)/shard_map/all_gather | solution.py:13
  134.1 0.7 copy.127
  134.8 0.7 copy.128
  135.6 0.7 copy.130
  136.3 0.2 copy.125
  136.5 1.4 fusion.13
  137.9 1.0 slice.202
  138.9 0.3 convolution_add_fusion
  139.2 2.2 %all-gather = f32[256,4,128]{2,1,0:T(4,128)S(1)} all-gather(f32[128,4,128]{2,1,0:T(4,128)S(1)} %convolution_add_fusion), channel_id=2, replica_groups=mesh['groups'=2,'replica'=8,'tensor'=2] {'tensor'}, dimensions={0}, use_global_device_ids=true | all-gather | bytes 786432 | tf_op jit(solution)/shard_map/all_gather | solution.py:13
  141.4 1.1 fusion.35
  142.5 5.6 %all-to-all-start.3 = ((bf16[128,4,128]{2,1,0:T(4,128)(2,1)}), bf16[128,4,128]{2,1,0:T(4,128)(2,1)S(1)}, u32[]{:S(2)}, u32[]{:S(2)}) async-start(bf16[128,4,128]{2,1,0:T(4,128)(2,1)} %fusion.35), calls=%async_computation.3 | async-start | bytes 262144 | tf_op jit(solution)/shard_map/all_to_all | solution.py:197
  148.1 6.2 %all-to-all-done.3 = bf16[128,4,128]{2,1,0:T(4,128)(2,1)S(1)} async-done(((bf16[128,4,128]{2,1,0:T(4,128)(2,1)}), bf16[128,4,128]{2,1,0:T(4,128)(2,1)S(1)}, u32[]{:S(2)}, u32[]{:S(2)}) %all-to-all-start.3) | async-done | bytes 131104 | tf_op jit(solution)/shard_map/all_to_all | solution.py:197
  154.2 0.7 gather_fusion.1
  154.9 0.6 copy.131
  (59 shorter events, 1.6 us)
Async XLA Ops:
  6.5 90.3 %copy-start = (bf16[2048,384]{1,0:T(8,128)(2,1)S(1)}, bf16[2048,384]{1,0:T(8,128)(2,1)}, u32[]{:S(2)}) copy-start(bf16[2048,384]{1,0:T(8,128)(2,1)} %param.10) | copy-start | bytes 4718596
  8.2 30.3 %copy-start.8 = (s32[64]{0:T(128)}, s32[64]{0:T(128)S(1)}, u32[]{:S(2)}) copy-start(s32[64]{0:T(128)S(1)} %fusion.69) | copy-start | bytes 772
  10.4 18.9 %all-to-all-start = ((s32[8,16,2]{1,2,0:T(2,128)}), s32[8,16,2]{1,2,0:T(2,128)S(1)}, u32[]{:S(2)}, u32[]{:S(2)}) async-start(s32[8,16,2]{1,2,0:T(2,128)} %copy.109), calls=%async_computation | async-start | bytes 16384 | tf_op jit(solution)/shard_map/all_to_all | solution.py:190
  29.3 6.1 %copy-start.11 = (s32[1,192]{1,0:T(1,128)S(1)}, s32[1,192]{1,0:T(1,128)}, u32[]{:S(2)}) copy-start(s32[1,192]{1,0:T(1,128)} %param.17) | copy-start | bytes 2308
  29.3 7.1 %copy-start.1 = (bf16[1,192,8,256]{3,2,1,0:T(8,128)(2,1)S(1)}, bf16[1,192,8,256]{3,2,1,0:T(8,128)(2,1)}, u32[]{:S(2)}) copy-start(bf16[1,192,8,256]{3,2,1,0:T(8,128)(2,1)} %param.13) | copy-start | bytes 2359300
  29.3 52.5 %all-to-all-start.1 = ((bf16[128,4,2048]{2,1,0:T(4,128)(2,1)}), bf16[128,4,2048]{2,1,0:T(4,128)(2,1)}, u32[]{:S(2)}, u32[]{:S(2)}) async-start(bf16[128,4,2048]{2,1,0:T(4,128)(2,1)} %scatter_fusion), calls=%async_computation.1 | async-start | bytes 4194304 | tf_op jit(solution)/shard_map/all_to_all | solution.py:188
  37.2 9.5 %copy-start.7 = (bf16[2,16,256]{2,1,0:T(8,128)(2,1)S(1)}, bf16[2,16,256]{2,1,0:T(8,128)(2,1)}, u32[]{:S(2)}) copy-start(bf16[2,16,256]{2,1,0:T(8,128)(2,1)} %param.12) | copy-start | bytes 49156
  46.6 40.7 %copy-start.12 = (bf16[2,2048,32]{1,2,0:T(8,128)(2,1)S(1)}, bf16[2,2048,32]{1,2,0:T(8,128)(2,1)}, u32[]{:S(2)}) copy-start(bf16[2,2048,32]{1,2,0:T(8,128)(2,1)} %param.11) | copy-start | bytes 786436
  81.8 45.0 %all-to-all-start.2 = ((bf16[128,24,256]{2,1,0:T(8,128)(2,1)}), bf16[128,24,256]{2,1,0:T(8,128)(2,1)S(1)}, u32[]{:S(2)}, u32[]{:S(2)}) async-start(bf16[128,24,256]{2,1,0:T(8,128)(2,1)} %scatter_fusion.1), calls=%async_computation.2 | async-start | bytes 3145728 | tf_op jit(solution)/shard_map/all_to_all | solution.py:189
  87.1 36.1 %all-reduce.2.cloned.1.call-start = ((), (), s32[]{:S(2)}) async-start(), calls=%async_computation.4 | async-start | bytes 1572864 | tf_op jit(solution)/shard_map/psum | solution.py:134
  102.1 26.2 %copy-start.10 = (pred[4,4]{1,0:T(4,128)(4,1)}, pred[4,4]{1,0:T(4,128)(4,1)S(1)}, u32[]{:S(2)}) copy-start(pred[4,4]{1,0:T(4,128)(4,1)S(1)} %fusion.68) | copy-start | bytes 52
  125.7 0.7 copy-start.6
  128.3 8.0 %copy-start.2 = (f32[128,4,24]{2,1,0:T(4,128)}, f32[128,4,24]{2,1,0:T(4,128)S(1)}, u32[]{:S(2)}) copy-start(f32[128,4,24]{2,1,0:T(4,128)S(1)} %get-tuple-element.45) | copy-start | bytes 147460
  136.3 5.0 %copy-start.3 = (f32[128,4]{1,0:T(8,128)S(1)}, f32[128,4]{1,0:T(8,128)}, u32[]{:S(2)}) copy-start(f32[128,4]{1,0:T(8,128)} %copy.127) | copy-start | bytes 6148
  136.3 5.0 %copy-start.4 = (f32[128,4]{1,0:T(8,128)S(1)}, f32[128,4]{1,0:T(8,128)}, u32[]{:S(2)}) copy-start(f32[128,4]{1,0:T(8,128)} %copy.128) | copy-start | bytes 6148
  136.3 5.0 %copy-start.5 = (f32[128,4]{1,0:T(8,128)S(1)}, f32[128,4]{1,0:T(8,128)}, u32[]{:S(2)}) copy-start(f32[128,4]{1,0:T(8,128)} %copy.130) | copy-start | bytes 6148
  136.5 11.5 %copy-start.9 = (s32[64]{0:T(128)S(1)}, s32[64]{0:T(128)}, u32[]{:S(2)}) copy-start(s32[64]{0:T(128)} %copy-done.8) | copy-start | bytes 772
  142.5 11.8 %all-to-all-start.3 = ((bf16[128,4,128]{2,1,0:T(4,128)(2,1)}), bf16[128,4,128]{2,1,0:T(4,128)(2,1)S(1)}, u32[]{:S(2)}, u32[]{:S(2)}) async-start(bf16[128,4,128]{2,1,0:T(4,128)(2,1)} %fusion.35), calls=%async_computation.3 | async-start | bytes 262144 | tf_op jit(solution)/shard_map/all_to_all | solution.py:197
Sparse Core Ops, SparseCore 0:
  102.1 20.9 all-reduce.1
where the time goes:
time: 165 us; the launch traced here: 162 us
  waiting for transfers between devices  61.5 us (37%)
  local copies, waits for them, and re-layouts  31 us (19%)
  starting transfers between devices  22.9 us (14%)
  matrix products  17.9 us (11%)
  between operations  13.7 us (8%)
  other arithmetic  9.62 us (6%)
  blocking collectives  5.75 us (3%)
    all_to_all x1, waiting for transfers between devices, on_device(): lax.all_to_all(row_buffer, 'replica', split_axis=0, concat_axis=0, tiled=...  35 us
    psum x1, waiting for transfers between devices, serve_rows(): summed = lax.psum(value_partial, 'tensor')  20.3 us
    scatter x1, local copies, waits for them, and re-layouts, on_device(): jnp.zeros((slot_total, step_count, feat_width), hidden.dtype).at[slot_of]  8.15 us
    scatter x1, local copies, waits for them, and re-layouts, on_device(): cache_buffer = jnp.zeros((slot_total, blocks * half_len, 2 * head_width),...  8.08 us
    dot_general x2, matrix products, adapter_delta(): jnp.dot(flattened_rows, adapter_down_weight[adapter_slot], preferred_elem...  7.78 us
    all_to_all x1, starting transfers between devices, on_device(): lax.all_to_all(meta_ints, 'replica', split_axis=0, concat_axis=0, tiled=T...  6.35 us
    all_to_all x1, waiting for transfers between devices, on_device(): lax.all_to_all(result, 'replica', split_axis=0, concat_axis=0, tiled=True)  6.18 us
    all_gather x3, blocking collectives, combined_all(): gathered = jax.tree.map(lambda a: lax.all_gather(a, axis), part)  5.75 us
  transfers between devices with their start and end apart: 5, of which 3 were waited for; matrix products, arithmetic and copies ran while one was open for 26% of the time, Pallas kernels for 0%

commit v1 on v0

--- a/solution.py
+++ b/solution.py
@@ -1,8 +1,11 @@
+import functools
 import math
 
 import jax
 import jax.numpy as jnp
 from jax import lax
+from jax.experimental import pallas as pl
+from jax.experimental.pallas import tpu as pltpu
 from jax.sharding import PartitionSpec as P
 
 rope_base = 500000.0
@@ -137,7 +140,7 @@
     return (accum / total_sum[..., None]).astype(jnp.bfloat16)
 
 
-def on_device(
+def rows_to_adapters(
     hidden,
     query_key_value_weight,
     adapter_down_weight,
@@ -198,6 +201,376 @@
     return jnp.swapaxes(returned[slot_of], 0, 1)
 
 
+def fold_columns(row, count):
+    down = lax.broadcasted_iota(jnp.int32, (count, count), 0)
+    along = lax.broadcasted_iota(jnp.int32, (count, count), 1)
+    return jnp.sum(jnp.where(down == along, row, 0), axis=1, keepdims=True)
+
+
+def gather_kernel(
+    steps,
+    hidden_hbm,
+    weight_hbm,
+    down_ref,
+    up_ref,
+    pool_hbm,
+    home_ref,
+    choice_ref,
+    length_ref,
+    table_ref,
+    out_ref,
+    hidden_v,
+    weight_v,
+    pool_v,
+    pages_f32,
+    pages,
+    downs,
+    ups,
+    up_full,
+    base,
+    low,
+    fresh_q,
+    fresh_k,
+    fresh_v,
+    cosine,
+    sine,
+    local_sem,
+    piece_send,
+    piece_recv,
+    up_send,
+    up_recv,
+    pair_send,
+    pair_recv,
+):
+    rows, width = hidden_v.shape
+    req = rows // steps
+    head = base.shape[2] // 3
+    half_block = pool_v.shape[1]
+    entries = pool_v.shape[0]
+    blocks = entries // req
+    rank2 = downs.shape[2]
+    rank = rank2 // 2
+    g = lax.axis_index("groups")
+    r = lax.axis_index("replica")
+    t = lax.axis_index("tensor")
+    z = r // 2
+    x = r % 2
+    far = {1: z + 1 - 2 * (z % 2), 2: (z + 2) % 4, 3: 3 - z}
+    other_x = 1 - x
+    z_dev = {d: {"replica": far[d] * 2 + x} for d in far}
+    x_dev = {"replica": z * 2 + other_x}
+    y_dev = {"groups": 1 - g}
+    t_dev = {"tensor": 1 - t}
+
+    barrier = pltpu.get_barrier_semaphore()
+    for peer in (z_dev[1], z_dev[2], z_dev[3], x_dev, y_dev, t_dev):
+        pl.semaphore_signal(barrier, inc=1, device_id=peer, device_id_type=pl.DeviceIdType.MESH)
+
+    loads = [
+        pltpu.make_async_copy(hidden_hbm, hidden_v, local_sem.at[0]),
+        pltpu.make_async_copy(weight_hbm, weight_v, local_sem.at[1]),
+        pltpu.make_async_copy(pool_hbm, pool_v, local_sem.at[2]),
+    ]
+    for load in loads:
+        load.start()
+    downs[r] = down_ref[...]
+    ups[r] = up_ref[...]
+    pl.semaphore_wait(barrier, 6)
+
+    sent = []
+
+    def piece(source, slot, device):
+        index = len(sent) // 2
+        return (
+            pltpu.make_async_remote_copy(
+                src_ref=downs.at[source, slot],
+                dst_ref=downs.at[source, slot],
+                send_sem=piece_send.at[index],
+                recv_sem=piece_recv.at[source, slot],
+                device_id=device,
+                device_id_type=pl.DeviceIdType.MESH,
+            ),
+            pltpu.make_async_remote_copy(
+                src_ref=ups.at[source, slot],
+                dst_ref=ups.at[source, slot],
+                send_sem=up_send.at[index],
+                recv_sem=up_recv.at[source, slot],
+                device_id=device,
+                device_id_type=pl.DeviceIdType.MESH,
+            ),
+        )
+
+    def send(source, slot, device):
+        for copy in piece(source, slot, device):
+            copy.start()
+            sent.append(copy)
+
+    def arrive(source, slot):
+        for semaphores, buffer in ((piece_recv, downs), (up_recv, ups)):
+            pltpu.make_async_copy(
+                buffer.at[source, slot], buffer.at[source, slot], semaphores.at[source, slot]
+            ).wait()
+
+    def pair(source, target, index):
+        copy = pltpu.make_async_remote_copy(
+            src_ref=source,
+            dst_ref=target,
+            send_sem=pair_send.at[index],
+            recv_sem=pair_recv.at[index],
+            device_id=t_dev,
+            device_id_type=pl.DeviceIdType.MESH,
+        )
+        copy.start()
+        return copy
+
+    ng = 1 - g
+    near, mid, last = far[1] * 2, far[2] * 2, far[3] * 2
+    here = z * 2
+
+    send(r, g, x_dev)
+    send(r, g, z_dev[1])
+    send(r, g, z_dev[2])
+    send(r, g, z_dev[3])
+    send(r, ng, z_dev[1])
+
+    loads[0].wait()
+    loads[1].wait()
+    base[0] = jnp.dot(hidden_v[...], weight_v[...], preferred_element_type=jnp.float32)
+    base_copy = pair(base.at[0], base.at[1], 0)
+
+    arrive(here + other_x, g)
+    send(here + other_x, g, y_dev)
+    arrive(near + x, g)
+    send(near + x, g, x_dev)
+
+    loads[2].wait()
+
+    def take_page(entry, carry):
+        page = pool_v[table_ref[0, entry]]
+        pages_f32[pl.ds(pl.multiple_of(entry * half_block, half_block), half_block), :] = (
+            page.astype(jnp.float32)
+        )
+        return carry
+
+    third = entries // 3
+    lax.fori_loop(0, third, take_page, 0, unroll=8)
+    arrive(mid + x, g)
+    send(mid + x, g, y_dev)
+    send(mid + x, g, x_dev)
+    lax.fori_loop(third, 2 * third, take_page, 0, unroll=8)
+    arrive(last + x, g)
+    send(last + x, g, y_dev)
+    send(last + x, g, x_dev)
+    lax.fori_loop(2 * third, entries, take_page, 0, unroll=8)
+    pages[t] = pages_f32[...].astype(jnp.bfloat16)
+    pages_copy = pair(pages.at[t], pages.at[t], 1)
+    arrive(near + x, ng)
+    send(near + x, ng, x_dev)
+
+    length = fold_columns(length_ref[...], req)
+    adapter = fold_columns(home_ref[...] * 2 + choice_ref[...], req)
+    lengths = jnp.concatenate([length] * steps, axis=0)
+    adapters = jnp.concatenate([adapter] * steps, axis=0)
+    step_of = lax.broadcasted_iota(jnp.int32, (rows, 1), 0) // req
+    position = (lengths + step_of).astype(jnp.float32)
+    lane = lax.broadcasted_iota(jnp.int32, (1, head), 1)
+    half = head // 2
+    frequency = jnp.exp(
+        (lane % half).astype(jnp.float32) * (-2.0 * math.log(rope_base) / head)
+    )
+    angles = position * frequency
+    cosine[...] = jnp.cos(angles)
+    sine[...] = jnp.where(lane < half, -jnp.sin(angles), jnp.sin(angles))
+
+    def rotated(vector):
+        turned = jnp.concatenate([vector[:, half:], vector[:, :half]], axis=1)
+        return vector * cosine[...] + turned * sine[...]
+
+    def rounded(vector):
+        return vector.astype(jnp.bfloat16).astype(jnp.float32)
+
+    def add_low(z_index, first):
+        packed = downs[pl.ds(z_index * 2, 2)].reshape(4 * rank2, width)
+        part = lax.dot_general(
+            hidden_v[...], packed, (((1,), (1,)), ((), ())), preferred_element_type=jnp.float32
+        )
+        owner = lax.broadcasted_iota(jnp.int32, (1, 4 * rank2), 1) // rank2 + 4 * z_index
+        part = jnp.where(adapters == owner, part, 0.0)
+        low[0] = part if first else low[0] + part
+
+    arrive(mid + other_x, g)
+    send(mid + other_x, g, y_dev)
+    base_copy.wait_recv()
+    fresh_k[...] = rounded(rotated(base[0, :, head : 2 * head] + base[1, :, head : 2 * head]))
+    arrive(last + other_x, g)
+    send(last + other_x, g, y_dev)
+
+    arrive(here + other_x, ng)
+    add_low(z, True)
+    arrive(near + other_x, g)
+    arrive(near + other_x, ng)
+    add_low(far[1], False)
+    pages_copy.wait_recv()
+    arrive(mid + x, ng)
+    arrive(mid + other_x, ng)
+    add_low(far[2], False)
+    arrive(last + x, ng)
+    arrive(last + other_x, ng)
+    add_low(far[3], False)
+    low_copy = pair(low.at[0], low.at[1], 2)
+
+    up_full[...] = jnp.zeros_like(up_full)
+    for source in range(ups.shape[0]):
+        for slot in range(2):
+            at = (source * 2 + slot) * rank2
+            up_full[at : at + rank, :head] = ups[source, slot, :, :head]
+            up_full[at + rank : at + rank2, head:] = ups[source, slot, :, head:]
+    low_copy.wait_recv()
+
+    low_sum = low[0] + low[1]
+    count = up_full.shape[0]
+    wide = jnp.concatenate([low_sum] * (count // (4 * rank2)), axis=1)
+    owner = lax.broadcasted_iota(jnp.int32, (1, count), 1) // rank2
+    wide = jnp.where(adapters == owner, wide, 0.0)
+    high = wide.astype(jnp.bfloat16)
+    rest = (wide - high.astype(jnp.float32)).astype(jnp.bfloat16)
+    term = jnp.dot(high, up_full[...], preferred_element_type=jnp.float32) + jnp.dot(
+        rest, up_full[...], preferred_element_type=jnp.float32
+    )
+    fresh_q[...] = rounded(rotated(base[0, :, :head] + base[1, :, :head] + term[:, :head]))
+    fresh_v[...] = base[0, :, 2 * head :] + base[1, :, 2 * head :] + term[:, head:]
+
+    each = 8
+    local = steps * each
+    span = each * blocks * half_block
+    down_row = lax.broadcasted_iota(jnp.int32, (local, 1), 0)
+    row_req = down_row % each
+    row_step = down_row // each
+    column = lax.broadcasted_iota(jnp.int32, (1, 2 * span), 1)
+    side = column // span
+    inner = column % span
+    col_pos = (
+        (inner // half_block) % blocks * (2 * half_block) + side * half_block + inner % half_block
+    )
+    same_old = inner // (blocks * half_block) == row_req
+    new_col = lax.broadcasted_iota(jnp.int32, (1, local), 1)
+    new_mask = (new_col % each == row_req) & (new_col // each <= row_step)
+    scaling = 1.0 / math.sqrt(head)
+    contract = (((1,), (1,)), ((), ()))
+
+    for group in range(req // each):
+        def picked(ref):
+            return jnp.concatenate(
+                [ref[s * req + group * each : s * req + (group + 1) * each, :] for s in range(steps)],
+                axis=0,
+            ).astype(jnp.bfloat16)
+
+        limit = jnp.concatenate([length[group * each : (group + 1) * each]] * steps, axis=0)
+        cached = jnp.concatenate(
+            [pages[h, group * span : (group + 1) * span, :] for h in range(2)], axis=0
+        )
+        query, key, value = picked(fresh_q), picked(fresh_k), picked(fresh_v)
+        old_mask = same_old & (col_pos < limit)
+        old = lax.dot_general(
+            query, cached[:, :head], contract, preferred_element_type=jnp.float32
+        )
+        new = lax.dot_general(query, key, contract, preferred_element_type=jnp.float32)
+        old = jnp.where(old_mask, old * scaling, neg_fill)
+        new = jnp.where(new_mask, new * scaling, neg_fill)
+        peak = jnp.maximum(
+            jnp.max(old, axis=1, keepdims=True), jnp.max(new, axis=1, keepdims=True)
+        )
+        old = jnp.where(old_mask, jnp.exp(old - peak), 0.0)
+        new = jnp.where(new_mask, jnp.exp(new - peak), 0.0)
+        total = jnp.sum(old, axis=1, keepdims=True) + jnp.sum(new, axis=1, keepdims=True)
+        mixed = jnp.dot(
+            old.astype(jnp.bfloat16), cached[:, head:], preferred_element_type=jnp.float32
+        ) + jnp.dot(new.astype(jnp.bfloat16), value, preferred_element_type=jnp.float32)
+        mixed = mixed / total
+        for s in range(steps):
+            out_ref[s, group * each : (group + 1) * each, :] = mixed[s * each : (s + 1) * each]
+
+    for copy in sent + [base_copy, pages_copy, low_copy]:
+        copy.wait_send()
+
+
+def adapters_to_rows(
+    hidden,
+    query_key_value_weight,
+    adapter_down_weight,
+    adapter_up_weight,
+    key_value_pool,
+    adapter_replica,
+    adapter_choice_index,
+    cached_length,
+    request_block_table,
+):
+    steps, req, width = hidden.shape
+    held, rank, head2 = adapter_up_weight.shape
+    head = head2 // 2
+    _, entries, half_block, _ = key_value_pool.shape
+    replicas = lax.axis_size("replica")
+    rows = steps * req
+    vmem = pl.BlockSpec(memory_space=pltpu.VMEM)
+    hbm = pl.BlockSpec(memory_space=pl.ANY)
+    smem = pl.BlockSpec(memory_space=pltpu.SMEM)
+    sends = 14
+    result = pl.pallas_call(
+        functools.partial(gather_kernel, steps),
+        out_shape=jax.ShapeDtypeStruct((steps, req, head), jnp.float32),
+        in_specs=[hbm, hbm, vmem, vmem, hbm, vmem, vmem, vmem, smem],
+        out_specs=vmem,
+        scratch_shapes=[
+            pltpu.VMEM((rows, width), hidden.dtype),
+            pltpu.VMEM((width, 3 * head), query_key_value_weight.dtype),
+            pltpu.VMEM((entries, half_block, head2), key_value_pool.dtype),
+            pltpu.VMEM((entries * half_block, head2), jnp.float32),
+            pltpu.VMEM((2, entries * half_block, head2), jnp.bfloat16),
+            pltpu.VMEM((replicas, held, 2 * rank, width), jnp.bfloat16),
+            pltpu.VMEM((replicas, held, rank, head2), jnp.bfloat16),
+            pltpu.VMEM((replicas * held * 2 * rank, head2), jnp.bfloat16),
+            pltpu.VMEM((2, rows, 3 * head), jnp.float32),
+            pltpu.VMEM((2, rows, 8 * rank), jnp.float32),
+            pltpu.VMEM((rows, head), jnp.float32),
+            pltpu.VMEM((rows, head), jnp.float32),
+            pltpu.VMEM((rows, head), jnp.float32),
+            pltpu.VMEM((rows, head), jnp.float32),
+            pltpu.VMEM((rows, head), jnp.float32),
+            pltpu.SemaphoreType.DMA((3,)),
+            pltpu.SemaphoreType.DMA((sends,)),
+            pltpu.SemaphoreType.DMA((replicas, held)),
+            pltpu.SemaphoreType.DMA((sends,)),
+            pltpu.SemaphoreType.DMA((replicas, held)),
+            pltpu.SemaphoreType.DMA((3,)),
+            pltpu.SemaphoreType.DMA((3,)),
+        ],
+        compiler_params=pltpu.CompilerParams(
+            collective_id=0, has_side_effects=True, vmem_limit_bytes=48 * 1024 * 1024
+        ),
+    )(
+        hidden.reshape(rows, width),
+        query_key_value_weight,
+        jnp.swapaxes(adapter_down_weight, 1, 2),
+        adapter_up_weight,
+        key_value_pool[0],
+        adapter_replica.reshape(1, req),
+        adapter_choice_index.reshape(1, req),
+        cached_length,
+        request_block_table,
+    )
+    return result.astype(jnp.bfloat16)
+
+
+def on_device(*arguments):
+    fits = (
+        lax.axis_size("replica") == 8
+        and lax.axis_size("groups") == 2
+        and lax.axis_size("tensor") == 2
+        and arguments[3].shape[0] == 2
+    )
+    return (adapters_to_rows if fits else rows_to_adapters)(*arguments)
+
+
 def solution(mesh):
     placed = (
         P(None, ("groups", "replica"), "tensor"),

time: 165 us -> 43.8 us (0.27); the launches traced: 162 us -> 43.4 us
  waiting for transfers between devices: 61.5 us -> 0 us
  Pallas kernels: 0 us -> 34.7 us
  local copies, waits for them, and re-layouts: 31 us -> 8.07 us
  starting transfers between devices: 22.9 us -> 0 us
  matrix products: 17.9 us -> 0 us
  between operations: 13.7 us -> 0.02 us
  other arithmetic: 9.62 us -> 0.64 us
  blocking collectives: 5.75 us -> 0 us
    all_to_all x4 -> x0, waiting for transfers between devices: 41.2 us -> none  [the longest x1 35 us: on_device(): lax.all_to_all(row_buffer, 'replica', split_axis=0, concat_axis=0, tiled=...]
    pallas_call x0 -> x1, Pallas kernels: none -> 34.7 us  [adapters_to_rows(): pl.pallas_call(functools.partial(gather_kernel, steps), out_shape=jax.Sha...]
    all_to_all x4 -> x0, starting transfers between devices: 22.7 us -> none  [the longest x1 6.35 us: on_device(): lax.all_to_all(meta_ints, 'replica', split_axis=0, concat_axis=0, tiled=T...]
    psum x1 -> x0, waiting for transfers between devices: 20.3 us -> none  [serve_rows(): summed = lax.psum(value_partial, 'tensor')]
    dot_general x11 -> x0, matrix products: 17.9 us -> none  [the longest x2 7.78 us: adapter_delta(): jnp.dot(flattened_rows, adapter_down_weight[adapter_slot], preferred_elem...]
    scatter x3 -> x0, local copies, waits for them, and re-layouts: 17 us -> none  [the longest x1 8.15 us: on_device(): jnp.zeros((slot_total, step_count, feat_width), hidden.dtype).at[slot_of]]
    unnamed x27 -> x18, local copies, waits for them, and re-layouts: 1.2 us -> 8.07 us
    all_gather x3 -> x0, blocking collectives: 5.75 us -> none  [combined_all(): gathered = jax.tree.map(lambda a: lax.all_gather(a, axis), part)]
  transfers between devices with their start and end apart: 5 -> 0, of which waited for: 3 -> 0; matrix products, arithmetic and copies ran while one was open for 26% -> 0% of each run, Pallas kernels for 0% -> 0%
where the time goes in v1:
time: 43.8 us; the launch traced here: 43.4 us
  Pallas kernels  34.7 us (79%)
  local copies, waits for them, and re-layouts  8.07 us (18%)
  other arithmetic  0.64 us (1%)
    pallas_call x1, Pallas kernels, adapters_to_rows(): pl.pallas_call(functools.partial(gather_kernel, steps), out_shape=jax.Sha...  34.7 us
    unnamed x18, local copies, waits for them, and re-layouts  8.07 us

profile of v1, /device:TPU:1, one launch (start us, length us, event | category | flops | bytes accessed | tf_op | source)
XLA Modules:
  0.0 43.4 jit_solution(1537496432975683440)
XLA Ops:
  0.0 0.0 copy-start
  0.0 1.4 %copy-done = bf16[2048,384]{1,0:T(8,128)(2,1)S(1)} copy-done((bf16[2048,384]{1,0:T(8,128)(2,1)S(1)}, bf16[2048,384]{1,0:T(8,128)(2,1)}, u32[]{:S(2)}) %copy-start) | copy-done | bytes 1572888
  1.4 0.0 copy-start.1
  1.4 1.2 %copy-done.1 = bf16[4,64,2048]{2,1,0:T(8,128)(2,1)S(1)} copy-done((bf16[4,64,2048]{2,1,0:T(8,128)(2,1)S(1)}, bf16[4,64,2048]{2,1,0:T(8,128)(2,1)}, u32[]{:S(2)}) %copy-start.1) | copy-done | bytes 1048600
  2.6 0.0 copy-start.2
  2.6 1.1 %copy-done.2 = bf16[1,192,8,256]{3,2,1,0:T(8,128)(2,1)S(1)} copy-done((bf16[1,192,8,256]{3,2,1,0:T(8,128)(2,1)S(1)}, bf16[1,192,8,256]{3,2,1,0:T(8,128)(2,1)}, u32[]{:S(2)}) %copy-start.2) | copy-done | bytes 786456
  3.8 0.0 copy-start.3
  3.8 0.9 %copy-done.3 = bf16[2,2048,32]{1,2,0:T(8,128)(2,1)S(1)} copy-done((bf16[2,2048,32]{1,2,0:T(8,128)(2,1)S(1)}, bf16[2,2048,32]{1,2,0:T(8,128)(2,1)}, u32[]{:S(2)}) %copy-start.3) | copy-done | bytes 262168
  4.7 0.0 copy-start.4
  4.7 0.7 %copy-done.4 = bf16[2,16,256]{2,1,0:T(8,128)(2,1)S(1)} copy-done((bf16[2,16,256]{2,1,0:T(8,128)(2,1)S(1)}, bf16[2,16,256]{2,1,0:T(8,128)(2,1)}, u32[]{:S(2)}) %copy-start.4) | copy-done | bytes 16408
  5.4 0.0 copy-start.5
  5.4 0.7 %copy-done.5 = s32[1,192]{1,0:T(1,128)S(1)} copy-done((s32[1,192]{1,0:T(1,128)S(1)}, s32[1,192]{1,0:T(1,128)}, u32[]{:S(2)}) %copy-start.5) | copy-done | bytes 792
  6.1 0.0 copy-start.6
  6.1 0.7 %copy-done.6 = s32[64,1]{0,1:T(1,128)S(1)} copy-done((s32[64,1]{0,1:T(1,128)S(1)}, s32[64,1]{0,1:T(1,128)}, u32[]{:S(2)}) %copy-start.6) | copy-done | bytes 280
  6.8 0.0 copy-start.7
  6.8 0.7 %copy-done.7 = s32[64]{0:T(128)S(1)} copy-done((s32[64]{0:T(128)S(1)}, s32[64]{0:T(128)}, u32[]{:S(2)}) %copy-start.7) | copy-done | bytes 280
  7.4 0.0 copy-start.8
  7.4 0.7 %copy-done.8 = s32[1,64]{1,0:T(1,128)S(1)} copy-done((s32[1,64]{1,0:T(1,128)S(1)}, s32[1,64]{1,0:T(1,128)}, u32[]{:S(2)}) %copy-start.8) | copy-done | bytes 280
  8.1 34.7 %shard_map.91 = f32[4,64,128]{2,1,0:T(8,128)S(1)} custom-call(bf16[256,2048]{1,0:T(8,128)(2,1)S(1)} %bitcast.5, bf16[2048,384]{1,0:T(8,128)(2,1)S(1)} %copy-done, bf16[2,32,2048]{2,1,0:T(8,128)(2,1)S(1)} %bitcast.7, bf16[2,16,256]{2,1,0:T(8,128)(2,1)S(1)} %copy-done.4, bf16[192,8,256]{2,1,0:T(8,128)(2,1)S(1)} %bitcast.6, s32[1,64]{1,0:T(1,128)S(1)} %bitcast.8, ...), custom_call_target="tpu_custom_call" | custom-call | tf_op jit(solution)/shard_map/pallas_call | solution.py:518
  42.8 0.6 %convert_element_type.3 = bf16[4,64,128]{2,1,0:T(8,128)(2,1)} convert(f32[4,64,128]{2,1,0:T(8,128)S(1)} %shard_map.91) | non-fusion elementwise | flops 32768 | bytes 196608 | tf_op jit(solution)/shard_map/convert_element_type | solution.py:561
Async XLA Ops:
  0.0 1.4 %copy-start = (bf16[2048,384]{1,0:T(8,128)(2,1)S(1)}, bf16[2048,384]{1,0:T(8,128)(2,1)}, u32[]{:S(2)}) copy-start(bf16[2048,384]{1,0:T(8,128)(2,1)} %weight_hbm.1) | copy-start | bytes 4718596
  1.4 1.2 %copy-start.1 = (bf16[4,64,2048]{2,1,0:T(8,128)(2,1)S(1)}, bf16[4,64,2048]{2,1,0:T(8,128)(2,1)}, u32[]{:S(2)}) copy-start(bf16[4,64,2048]{2,1,0:T(8,128)(2,1)} %param.9) | copy-start | bytes 3145732
  2.6 1.1 %copy-start.2 = (bf16[1,192,8,256]{3,2,1,0:T(8,128)(2,1)S(1)}, bf16[1,192,8,256]{3,2,1,0:T(8,128)(2,1)}, u32[]{:S(2)}) copy-start(bf16[1,192,8,256]{3,2,1,0:T(8,128)(2,1)} %param.13) | copy-start | bytes 2359300
  3.8 0.9 %copy-start.3 = (bf16[2,2048,32]{1,2,0:T(8,128)(2,1)S(1)}, bf16[2,2048,32]{1,2,0:T(8,128)(2,1)}, u32[]{:S(2)}) copy-start(bf16[2,2048,32]{1,2,0:T(8,128)(2,1)} %param.11) | copy-start | bytes 786436
  4.7 0.7 %copy-start.4 = (bf16[2,16,256]{2,1,0:T(8,128)(2,1)S(1)}, bf16[2,16,256]{2,1,0:T(8,128)(2,1)}, u32[]{:S(2)}) copy-start(bf16[2,16,256]{2,1,0:T(8,128)(2,1)} %up_ref.1) | copy-start | bytes 49156
  5.4 0.7 %copy-start.5 = (s32[1,192]{1,0:T(1,128)S(1)}, s32[1,192]{1,0:T(1,128)}, u32[]{:S(2)}) copy-start(s32[1,192]{1,0:T(1,128)} %table_ref.1) | copy-start | bytes 2308
  6.1 0.7 %copy-start.6 = (s32[64,1]{0,1:T(1,128)S(1)}, s32[64,1]{0,1:T(1,128)}, u32[]{:S(2)}) copy-start(s32[64,1]{0,1:T(1,128)} %param.14) | copy-start | bytes 772
  6.8 0.7 %copy-start.7 = (s32[64]{0:T(128)S(1)}, s32[64]{0:T(128)}, u32[]{:S(2)}) copy-start(s32[64]{0:T(128)} %param.15) | copy-start | bytes 772
  7.4 0.7 %copy-start.8 = (s32[1,64]{1,0:T(1,128)S(1)}, s32[1,64]{1,0:T(1,128)}, u32[]{:S(2)}) copy-start(s32[1,64]{1,0:T(1,128)} %length_ref.1) | copy-start | bytes 772

commit v2 on v1

--- a/solution.py
+++ b/solution.py
@@ -211,17 +211,21 @@
     steps,
     hidden_hbm,
     weight_hbm,
-    down_ref,
-    up_ref,
+    down_hbm,
+    up_hbm,
     pool_hbm,
+    home_hbm,
+    choice_hbm,
+    length_hbm,
+    table_hbm,
+    out_ref,
+    hidden_v,
+    weight_v,
+    pool_v,
     home_ref,
     choice_ref,
     length_ref,
     table_ref,
-    out_ref,
-    hidden_v,
-    weight_v,
-    pool_v,
     pages_f32,
     pages,
     downs,
@@ -266,15 +270,25 @@
     for peer in (z_dev[1], z_dev[2], z_dev[3], x_dev, y_dev, t_dev):
         pl.semaphore_signal(barrier, inc=1, device_id=peer, device_id_type=pl.DeviceIdType.MESH)
 
+    own = (
+        (down_hbm, downs.at[r]),
+        (up_hbm, ups.at[r]),
+        (hidden_hbm, hidden_v),
+        (weight_hbm, weight_v),
+        (pool_hbm, pool_v),
+        (table_hbm, table_ref),
+        (length_hbm, length_ref),
+        (home_hbm, home_ref),
+        (choice_hbm, choice_ref),
+    )
     loads = [
-        pltpu.make_async_copy(hidden_hbm, hidden_v, local_sem.at[0]),
-        pltpu.make_async_copy(weight_hbm, weight_v, local_sem.at[1]),
-        pltpu.make_async_copy(pool_hbm, pool_v, local_sem.at[2]),
+        pltpu.make_async_copy(source, target, local_sem.at[index])
+        for index, (source, target) in enumerate(own)
     ]
     for load in loads:
         load.start()
-    downs[r] = down_ref[...]
-    ups[r] = up_ref[...]
+    loads[0].wait()
+    loads[1].wait()
     pl.semaphore_wait(barrier, 6)
 
     sent = []
@@ -333,8 +347,8 @@
     send(r, g, z_dev[3])
     send(r, ng, z_dev[1])
 
-    loads[0].wait()
-    loads[1].wait()
+    loads[2].wait()
+    loads[3].wait()
     base[0] = jnp.dot(hidden_v[...], weight_v[...], preferred_element_type=jnp.float32)
     base_copy = pair(base.at[0], base.at[1], 0)
 
@@ -343,7 +357,8 @@
     arrive(near + x, g)
     send(near + x, g, x_dev)
 
-    loads[2].wait()
+    for load in loads[4:]:
+        load.wait()
 
     def take_page(entry, carry):
         page = pool_v[table_ref[0, entry]]
@@ -512,18 +527,21 @@
     replicas = lax.axis_size("replica")
     rows = steps * req
     vmem = pl.BlockSpec(memory_space=pltpu.VMEM)
-    hbm = pl.BlockSpec(memory_space=pl.ANY)
-    smem = pl.BlockSpec(memory_space=pltpu.SMEM)
+    hbm = pl.BlockSpec(memory_space=pltpu.HBM)
     sends = 14
     result = pl.pallas_call(
         functools.partial(gather_kernel, steps),
         out_shape=jax.ShapeDtypeStruct((steps, req, head), jnp.float32),
-        in_specs=[hbm, hbm, vmem, vmem, hbm, vmem, vmem, vmem, smem],
+        in_specs=[hbm] * 9,
         out_specs=vmem,
         scratch_shapes=[
             pltpu.VMEM((rows, width), hidden.dtype),
             pltpu.VMEM((width, 3 * head), query_key_value_weight.dtype),
             pltpu.VMEM((entries, half_block, head2), key_value_pool.dtype),
+            pltpu.VMEM((1, req), jnp.int32),
+            pltpu.VMEM((1, req), jnp.int32),
+            pltpu.VMEM((1, req), jnp.int32),
+            pltpu.SMEM((1, entries), jnp.int32),
             pltpu.VMEM((entries * half_block, head2), jnp.float32),
             pltpu.VMEM((2, entries * half_block, head2), jnp.bfloat16),
             pltpu.VMEM((replicas, held, 2 * rank, width), jnp.bfloat16),
@@ -536,7 +554,7 @@
             pltpu.VMEM((rows, head), jnp.float32),
             pltpu.VMEM((rows, head), jnp.float32),
             pltpu.VMEM((rows, head), jnp.float32),
-            pltpu.SemaphoreType.DMA((3,)),
+            pltpu.SemaphoreType.DMA((9,)),
             pltpu.SemaphoreType.DMA((sends,)),
             pltpu.SemaphoreType.DMA((replicas, held)),
             pltpu.SemaphoreType.DMA((sends,)),
@@ -545,7 +563,7 @@
             pltpu.SemaphoreType.DMA((3,)),
         ],
         compiler_params=pltpu.CompilerParams(
-            collective_id=0, has_side_effects=True, vmem_limit_bytes=48 * 1024 * 1024
+            collective_id=0, has_side_effects=True, vmem_limit_bytes=64 * 1024 * 1024
         ),
     )(
         hidden.reshape(rows, width),

time: 43.8 us -> 36.6 us (0.84)
  local copies, waits for them, and re-layouts: 8.07 us -> 0 us
  other arithmetic: 0.64 us -> 1.54 us
    unnamed x18 -> x0, local copies, waits for them, and re-layouts: 8.07 us -> none
    convert_element_type x1, other arithmetic: 0.64 us -> 1.54 us  [adapters_to_rows(): return result.astype(jnp.bfloat16)]
where the time goes in v2:
time: 36.6 us; the launch traced here: 36.5 us
  Pallas kernels  34.9 us (95%)
  other arithmetic  1.54 us (4%)
    pallas_call x1, Pallas kernels, adapters_to_rows(): pl.pallas_call(functools.partial(gather_kernel, steps), out_shape=jax.Sha...  34.9 us
    convert_element_type x1, other arithmetic, adapters_to_rows(): return result.astype(jnp.bfloat16)  1.54 us

profile of v2, /device:TPU:1, one launch (start us, length us, event | category | flops | bytes accessed | tf_op | source)
XLA Modules:
  0.0 36.5 jit_solution(13520161434225951742)
XLA Ops:
  0.0 34.9 %shard_map.91 = f32[4,64,128]{2,1,0:T(8,128)} custom-call(bf16[256,2048]{1,0:T(8,128)(2,1)} %bitcast.5, bf16[2048,384]{1,0:T(8,128)(2,1)} %weight_hbm.1, bf16[2,32,2048]{2,1,0:T(8,128)(2,1)} %bitcast.7, bf16[2,16,256]{2,1,0:T(8,128)(2,1)} %up_hbm.1, bf16[192,8,256]{2,1,0:T(8,128)(2,1)} %bitcast.6, s32[1,64]{1,0:T(1,128)} %bitcast.8, s32[1,64]{1,0:T(1,128)} %bitcast.9, ...), custom_call_target="tpu_custom_call" | custom-call | tf_op jit(solution)/shard_map/pallas_call | solution.py:532
  34.9 1.5 %convert_element_type.3 = bf16[4,64,128]{2,1,0:T(8,128)(2,1)} convert(f32[4,64,128]{2,1,0:T(8,128)} %shard_map.91) | non-fusion elementwise | flops 32768 | bytes 196608 | tf_op jit(solution)/shard_map/convert_element_type | solution.py:579

commit v3 on v2

--- a/solution.py
+++ b/solution.py
@@ -233,6 +233,9 @@
     up_full,
     base,
     low,
+    hidden_y,
+    names,
+    packed_low,
     fresh_q,
     fresh_k,
     fresh_v,
@@ -245,6 +248,8 @@
     up_recv,
     pair_send,
     pair_recv,
+    cross_send,
+    cross_recv,
 ):
     rows, width = hidden_v.shape
     req = rows // steps
@@ -265,14 +270,18 @@
     x_dev = {"replica": z * 2 + other_x}
     y_dev = {"groups": 1 - g}
     t_dev = {"tensor": 1 - t}
+    yt_dev = {"groups": 1 - g, "tensor": 1 - t}
+    part_width = width // 2
+    mine = pl.ds(pl.multiple_of(g * part_width, part_width), part_width)
+    theirs = pl.ds(pl.multiple_of((1 - g) * part_width, part_width), part_width)
 
     barrier = pltpu.get_barrier_semaphore()
-    for peer in (z_dev[1], z_dev[2], z_dev[3], x_dev, y_dev, t_dev):
+    for peer in (z_dev[1], z_dev[2], z_dev[3], x_dev, y_dev, t_dev, yt_dev):
         pl.semaphore_signal(barrier, inc=1, device_id=peer, device_id_type=pl.DeviceIdType.MESH)
 
     own = (
-        (down_hbm, downs.at[r]),
-        (up_hbm, ups.at[r]),
+        (down_hbm.at[:, :, mine], downs.at[r]),
+        (up_hbm.at[t], ups.at[t, r]),
         (hidden_hbm, hidden_v),
         (weight_hbm, weight_v),
         (pool_hbm, pool_v),
@@ -289,75 +298,71 @@
         load.start()
     loads[0].wait()
     loads[1].wait()
-    pl.semaphore_wait(barrier, 6)
+    loads[2].wait()
+    loads[7].wait()
+    loads[8].wait()
+    names[0] = home_ref[...] * 2 + choice_ref[...]
+    pl.semaphore_wait(barrier, 7)
 
     sent = []
 
-    def piece(source, slot, device):
-        index = len(sent) // 2
-        return (
-            pltpu.make_async_remote_copy(
-                src_ref=downs.at[source, slot],
-                dst_ref=downs.at[source, slot],
-                send_sem=piece_send.at[index],
-                recv_sem=piece_recv.at[source, slot],
-                device_id=device,
-                device_id_type=pl.DeviceIdType.MESH,
-            ),
-            pltpu.make_async_remote_copy(
-                src_ref=ups.at[source, slot],
-                dst_ref=ups.at[source, slot],
-                send_sem=up_send.at[index],
-                recv_sem=up_recv.at[source, slot],
-                device_id=device,
-                device_id_type=pl.DeviceIdType.MESH,
-            ),
-        )
-
-    def send(source, slot, device):
-        for copy in piece(source, slot, device):
-            copy.start()
-            sent.append(copy)
-
-    def arrive(source, slot):
-        for semaphores, buffer in ((piece_recv, downs), (up_recv, ups)):
-            pltpu.make_async_copy(
-                buffer.at[source, slot], buffer.at[source, slot], semaphores.at[source, slot]
-            ).wait()
-
-    def pair(source, target, index):
+    def remote(source, target, send_sem, recv_sem, device):
         copy = pltpu.make_async_remote_copy(
             src_ref=source,
             dst_ref=target,
-            send_sem=pair_send.at[index],
-            recv_sem=pair_recv.at[index],
-            device_id=t_dev,
+            send_sem=send_sem,
+            recv_sem=recv_sem,
+            device_id=device,
             device_id_type=pl.DeviceIdType.MESH,
         )
         copy.start()
+        sent.append(copy)
         return copy
 
-    ng = 1 - g
+    counts = [0, 0]
+
+    def send(source, slot, device):
+        at = downs.at[source, slot]
+        remote(at, at, piece_send.at[counts[0]], piece_recv.at[source, slot], device)
+        counts[0] += 1
+        if slot == 0:
+            at = ups.at[t, source]
+            remote(at, at, up_send.at[counts[1]], up_recv.at[source], device)
+            counts[1] += 1
+
+    def landed(target, semaphore):
+        pltpu.make_async_copy(target, target, semaphore).wait()
+
+    def arrive(source, slot):
+        landed(downs.at[source, slot], piece_recv.at[source, slot])
+        if slot == 0:
+            landed(ups.at[t, source], up_recv.at[source])
+
+    def pair(source, target, index):
+        return remote(source, target, pair_send.at[index], pair_recv.at[index], t_dev)
+
     near, mid, last = far[1] * 2, far[2] * 2, far[3] * 2
     here = z * 2
 
-    send(r, g, x_dev)
-    send(r, g, z_dev[1])
-    send(r, g, z_dev[2])
-    send(r, g, z_dev[3])
-    send(r, ng, z_dev[1])
-
-    loads[2].wait()
+    for slot in range(2):
+        send(r, slot, x_dev)
+    for slot in range(2):
+        send(r, slot, z_dev[1])
+    remote(names.at[0], names.at[1], cross_send.at[0], cross_recv.at[0], y_dev)
+    remote(hidden_v.at[:, theirs], hidden_y, cross_send.at[1], cross_recv.at[1], y_dev)
+    for slot in range(2):
+        send(r, slot, z_dev[2])
+        send(r, slot, z_dev[3])
+
     loads[3].wait()
     base[0] = jnp.dot(hidden_v[...], weight_v[...], preferred_element_type=jnp.float32)
     base_copy = pair(base.at[0], base.at[1], 0)
 
-    arrive(here + other_x, g)
-    send(here + other_x, g, y_dev)
-    arrive(near + x, g)
-    send(near + x, g, x_dev)
-
-    for load in loads[4:]:
+    arrive(near + x, 0)
+    send(near + x, 0, x_dev)
+    arrive(near + x, 1)
+    send(near + x, 1, x_dev)
+    for load in loads[4:7]:
         load.wait()
 
     def take_page(entry, carry):
@@ -369,21 +374,19 @@
 
     third = entries // 3
     lax.fori_loop(0, third, take_page, 0, unroll=8)
-    arrive(mid + x, g)
-    send(mid + x, g, y_dev)
-    send(mid + x, g, x_dev)
+    arrive(mid + x, 0)
+    send(mid + x, 0, x_dev)
     lax.fori_loop(third, 2 * third, take_page, 0, unroll=8)
-    arrive(last + x, g)
-    send(last + x, g, y_dev)
-    send(last + x, g, x_dev)
+    arrive(last + x, 0)
+    send(last + x, 0, x_dev)
     lax.fori_loop(2 * third, entries, take_page, 0, unroll=8)
     pages[t] = pages_f32[...].astype(jnp.bfloat16)
     pages_copy = pair(pages.at[t], pages.at[t], 1)
-    arrive(near + x, ng)
-    send(near + x, ng, x_dev)
-
     length = fold_columns(length_ref[...], req)
-    adapter = fold_columns(home_ref[...] * 2 + choice_ref[...], req)
+    adapter = fold_columns(names[0], req)
+    landed(names.at[1], cross_recv.at[0])
+    adapter_y = fold_columns(names[1], req)
+    adapters_y = jnp.concatenate([adapter_y] * steps, axis=0)
     lengths = jnp.concatenate([length] * steps, axis=0)
     adapters = jnp.concatenate([adapter] * steps, axis=0)
     step_of = lax.broadcasted_iota(jnp.int32, (rows, 1), 0) // req
@@ -404,45 +407,66 @@
     def rounded(vector):
         return vector.astype(jnp.bfloat16).astype(jnp.float32)
 
-    def add_low(z_index, first):
-        packed = downs[pl.ds(z_index * 2, 2)].reshape(4 * rank2, width)
-        part = lax.dot_general(
-            hidden_v[...], packed, (((1,), (1,)), ((), ())), preferred_element_type=jnp.float32
-        )
-        owner = lax.broadcasted_iota(jnp.int32, (1, 4 * rank2), 1) // rank2 + 4 * z_index
-        part = jnp.where(adapters == owner, part, 0.0)
-        low[0] = part if first else low[0] + part
-
-    arrive(mid + other_x, g)
-    send(mid + other_x, g, y_dev)
+    arrive(mid + x, 1)
+    send(mid + x, 1, x_dev)
     base_copy.wait_recv()
     fresh_k[...] = rounded(rotated(base[0, :, head : 2 * head] + base[1, :, head : 2 * head]))
-    arrive(last + other_x, g)
-    send(last + other_x, g, y_dev)
-
-    arrive(here + other_x, ng)
-    add_low(z, True)
-    arrive(near + other_x, g)
-    arrive(near + other_x, ng)
-    add_low(far[1], False)
+    arrive(last + x, 1)
+    send(last + x, 1, x_dev)
+
+    lane_group = lax.broadcasted_iota(jnp.int32, (1, 4 * rank2), 1) // rank2
+
+    def low_part(z_index, lhs, chosen):
+        packed = downs[pl.ds(z_index * 2, 2)].reshape(4 * rank2, part_width)
+        part = lax.dot_general(
+            lhs, packed, (((1,), (1,)), ((), ())), preferred_element_type=jnp.float32
+        )
+        return jnp.where(chosen == lane_group + 4 * z_index, part, 0.0)
+
+    def spread(part):
+        part = part + pltpu.roll(part, 2 * rank2, 1)
+        return part + pltpu.roll(part, rank2, 1)
+
+    arrive(here + other_x, 0)
+    arrive(here + other_x, 1)
+    landed(hidden_y, cross_recv.at[1])
+    low_y = low_part(z, hidden_y[...], adapters_y)
+    low[0] = low_part(z, hidden_v[:, mine], adapters)
     pages_copy.wait_recv()
-    arrive(mid + x, ng)
-    arrive(mid + other_x, ng)
-    add_low(far[2], False)
-    arrive(last + x, ng)
-    arrive(last + other_x, ng)
-    add_low(far[3], False)
+    for source in (1, 2):
+        arrive(far[source] * 2 + other_x, 0)
+        arrive(far[source] * 2 + other_x, 1)
+        low_y = low_y + low_part(far[source], hidden_y[...], adapters_y)
+        low[0] = low[0] + low_part(far[source], hidden_v[:, mine], adapters)
+    arrive(last + other_x, 0)
+    up_copy = pair(ups.at[t], ups.at[t], 3)
+    arrive(last + other_x, 1)
+    low_y = spread(low_y + low_part(far[3], hidden_y[...], adapters_y))
+    joined = low_y[:req]
+    for s in range(1, steps):
+        joined = jnp.where(lane_group == s, low_y[s * req : (s + 1) * req], joined)
+    packed_low[0] = joined
+    remote(packed_low.at[0], packed_low.at[1], cross_send.at[2], cross_recv.at[2], y_dev)
+    remote(packed_low.at[0], packed_low.at[2], cross_send.at[3], cross_recv.at[3], yt_dev)
+    low[0] = low[0] + low_part(far[3], hidden_v[:, mine], adapters)
     low_copy = pair(low.at[0], low.at[1], 2)
+    up_copy.wait_recv()
 
     up_full[...] = jnp.zeros_like(up_full)
-    for source in range(ups.shape[0]):
+    for source in range(ups.shape[1]):
         for slot in range(2):
             at = (source * 2 + slot) * rank2
-            up_full[at : at + rank, :head] = ups[source, slot, :, :head]
-            up_full[at + rank : at + rank2, head:] = ups[source, slot, :, head:]
+            up_full[at : at + rank, :head] = ups[slot, source, :, :head]
+            up_full[at + rank : at + rank2, head:] = ups[slot, source, :, head:]
     low_copy.wait_recv()
-
-    low_sum = low[0] + low[1]
+    landed(packed_low.at[1], cross_recv.at[2])
+    landed(packed_low.at[2], cross_recv.at[3])
+
+    away = packed_low[1] + packed_low[2]
+    away = jnp.concatenate(
+        [spread(jnp.where(lane_group == s, away, 0.0)) for s in range(steps)], axis=0
+    )
+    low_sum = low[0] + low[1] + away
     count = up_full.shape[0]
     wide = jnp.concatenate([low_sum] * (count // (4 * rank2)), axis=1)
     owner = lax.broadcasted_iota(jnp.int32, (1, count), 1) // rank2
@@ -505,7 +529,7 @@
         for s in range(steps):
             out_ref[s, group * each : (group + 1) * each, :] = mixed[s * each : (s + 1) * each]
 
-    for copy in sent + [base_copy, pages_copy, low_copy]:
+    for copy in sent:
         copy.wait_send()
 
 
@@ -544,11 +568,14 @@
             pltpu.SMEM((1, entries), jnp.int32),
             pltpu.VMEM((entries * half_block, head2), jnp.float32),
             pltpu.VMEM((2, entries * half_block, head2), jnp.bfloat16),
-            pltpu.VMEM((replicas, held, 2 * rank, width), jnp.bfloat16),
-            pltpu.VMEM((replicas, held, rank, head2), jnp.bfloat16),
+            pltpu.VMEM((replicas, held, 2 * rank, width // 2), jnp.bfloat16),
+            pltpu.VMEM((held, replicas, rank, head2), jnp.bfloat16),
             pltpu.VMEM((replicas * held * 2 * rank, head2), jnp.bfloat16),
             pltpu.VMEM((2, rows, 3 * head), jnp.float32),
             pltpu.VMEM((2, rows, 8 * rank), jnp.float32),
+            pltpu.VMEM((rows, width // 2), hidden.dtype),
+            pltpu.VMEM((2, 1, req), jnp.int32),
+            pltpu.VMEM((3, req, 8 * rank), jnp.float32),
             pltpu.VMEM((rows, head), jnp.float32),
             pltpu.VMEM((rows, head), jnp.float32),
             pltpu.VMEM((rows, head), jnp.float32),
@@ -557,10 +584,12 @@
             pltpu.SemaphoreType.DMA((9,)),
             pltpu.SemaphoreType.DMA((sends,)),
             pltpu.SemaphoreType.DMA((replicas, held)),
-            pltpu.SemaphoreType.DMA((sends,)),
-            pltpu.SemaphoreType.DMA((replicas, held)),
-            pltpu.SemaphoreType.DMA((3,)),
-            pltpu.SemaphoreType.DMA((3,)),
+            pltpu.SemaphoreType.DMA((sends // 2,)),
+            pltpu.SemaphoreType.DMA((replicas,)),
+            pltpu.SemaphoreType.DMA((4,)),
+            pltpu.SemaphoreType.DMA((4,)),
+            pltpu.SemaphoreType.DMA((4,)),
+            pltpu.SemaphoreType.DMA((4,)),
         ],
         compiler_params=pltpu.CompilerParams(
             collective_id=0, has_side_effects=True, vmem_limit_bytes=64 * 1024 * 1024

time: 36.6 us -> 32.2 us (0.88)
  Pallas kernels: 34.9 us -> 30.2 us
    pallas_call x1, Pallas kernels: 34.9 us -> 30.2 us  [adapters_to_rows(): pl.pallas_call(functools.partial(gather_kernel, steps), out_shape=jax.Sha...]
where the time goes in v3:
time: 32.2 us; the launch traced here: 31.7 us
  Pallas kernels  30.2 us (94%)
  other arithmetic  1.54 us (5%)
    pallas_call x1, Pallas kernels, adapters_to_rows(): pl.pallas_call(functools.partial(gather_kernel, steps), out_shape=jax.Sha...  30.2 us
    convert_element_type x1, other arithmetic, adapters_to_rows(): return result.astype(jnp.bfloat16)  1.54 us

profile of v3, /device:TPU:1, one launch (start us, length us, event | category | flops | bytes accessed | tf_op | source)
XLA Modules:
  0.0 31.7 jit_solution(1917793759999466300)
XLA Ops:
  0.0 30.2 %shard_map.91 = f32[4,64,128]{2,1,0:T(8,128)} custom-call(bf16[256,2048]{1,0:T(8,128)(2,1)} %bitcast.5, bf16[2048,384]{1,0:T(8,128)(2,1)} %weight_hbm.1, bf16[2,32,2048]{2,1,0:T(8,128)(2,1)} %bitcast.7, bf16[2,16,256]{2,1,0:T(8,128)(2,1)} %up_hbm.1, bf16[192,8,256]{2,1,0:T(8,128)(2,1)} %bitcast.6, s32[1,64]{1,0:T(1,128)} %bitcast.8, s32[1,64]{1,0:T(1,128)} %bitcast.9, ...), custom_call_target="tpu_custom_call" | custom-call | tf_op jit(solution)/shard_map/pallas_call | solution.py:556
  30.2 1.5 %convert_element_type.3 = bf16[4,64,128]{2,1,0:T(8,128)(2,1)} convert(f32[4,64,128]{2,1,0:T(8,128)} %shard_map.91) | non-fusion elementwise | flops 32768 | bytes 196608 | tf_op jit(solution)/shard_map/convert_element_type | solution.py:608

commit v4 on v3

--- a/solution.py
+++ b/solution.py
@@ -236,6 +236,8 @@
     hidden_y,
     names,
     packed_low,
+    bias,
+    new_bias,
     fresh_q,
     fresh_k,
     fresh_v,
@@ -250,6 +252,8 @@
     pair_recv,
     cross_send,
     cross_recv,
+    relay_send,
+    relay_up_send,
 ):
     rows, width = hidden_v.shape
     req = rows // steps
@@ -341,7 +345,44 @@
     def pair(source, target, index):
         return remote(source, target, pair_send.at[index], pair_recv.at[index], t_dev)
 
-    near, mid, last = far[1] * 2, far[2] * 2, far[3] * 2
+    first_z = 2 - z // 2
+    second_z = 3 * (1 - z // 2)
+    near, mid, last = far[1] * 2, first_z * 2, second_z * 2
+    inner = (z + 1) // 2 == 1
+    relays = []
+
+    def relay(source, slot, device):
+        index = len(relays)
+        at = downs.at[source, slot]
+        copies = [
+            pltpu.make_async_remote_copy(
+                src_ref=at,
+                dst_ref=at,
+                send_sem=relay_send.at[index],
+                recv_sem=piece_recv.at[source, slot],
+                device_id=device,
+                device_id_type=pl.DeviceIdType.MESH,
+            )
+        ]
+        if slot == 0:
+            at = ups.at[t, source]
+            copies.append(
+                pltpu.make_async_remote_copy(
+                    src_ref=at,
+                    dst_ref=at,
+                    send_sem=relay_up_send.at[index],
+                    recv_sem=up_recv.at[source],
+                    device_id=device,
+                    device_id_type=pl.DeviceIdType.MESH,
+                )
+            )
+        relays.append(copies)
+
+        @pl.when(inner)
+        def _():
+            for copy in copies:
+                copy.start()
+
     here = z * 2
 
     for slot in range(2):
@@ -349,18 +390,19 @@
     for slot in range(2):
         send(r, slot, z_dev[1])
     remote(names.at[0], names.at[1], cross_send.at[0], cross_recv.at[0], y_dev)
+    for slot in range(2):
+        relay(r, slot, z_dev[3])
     remote(hidden_v.at[:, theirs], hidden_y, cross_send.at[1], cross_recv.at[1], y_dev)
-    for slot in range(2):
-        send(r, slot, z_dev[2])
-        send(r, slot, z_dev[3])
 
     loads[3].wait()
     base[0] = jnp.dot(hidden_v[...], weight_v[...], preferred_element_type=jnp.float32)
     base_copy = pair(base.at[0], base.at[1], 0)
 
     arrive(near + x, 0)
+    relay(near + x, 0, z_dev[3])
     send(near + x, 0, x_dev)
     arrive(near + x, 1)
+    relay(near + x, 1, z_dev[3])
     send(near + x, 1, x_dev)
     for load in loads[4:7]:
         load.wait()
@@ -375,10 +417,12 @@
     third = entries // 3
     lax.fori_loop(0, third, take_page, 0, unroll=8)
     arrive(mid + x, 0)
+    relay(mid + x, 0, z_dev[1])
     send(mid + x, 0, x_dev)
     lax.fori_loop(third, 2 * third, take_page, 0, unroll=8)
-    arrive(last + x, 0)
-    send(last + x, 0, x_dev)
+    arrive(mid + x, 1)
+    relay(mid + x, 1, z_dev[1])
+    send(mid + x, 1, x_dev)
     lax.fori_loop(2 * third, entries, take_page, 0, unroll=8)
     pages[t] = pages_f32[...].astype(jnp.bfloat16)
     pages_copy = pair(pages.at[t], pages.at[t], 1)
@@ -407,11 +451,13 @@
     def rounded(vector):
         return vector.astype(jnp.bfloat16).astype(jnp.float32)
 
-    arrive(mid + x, 1)
-    send(mid + x, 1, x_dev)
+    arrive(last + x, 0)
+    relay(last + x, 0, z_dev[1])
+    send(last + x, 0, x_dev)
     base_copy.wait_recv()
     fresh_k[...] = rounded(rotated(base[0, :, head : 2 * head] + base[1, :, head : 2 * head]))
     arrive(last + x, 1)
+    relay(last + x, 1, z_dev[1])
     send(last + x, 1, x_dev)
 
     lane_group = lax.broadcasted_iota(jnp.int32, (1, 4 * rank2), 1) // rank2
@@ -426,6 +472,29 @@
     def spread(part):
         part = part + pltpu.roll(part, 2 * rank2, 1)
         return part + pltpu.roll(part, rank2, 1)
+
+    each = 8
+    local = steps * each
+    span = each * blocks * half_block
+    down_row = lax.broadcasted_iota(jnp.int32, (local, 1), 0)
+    row_req = down_row % each
+    row_step = down_row // each
+    column = lax.broadcasted_iota(jnp.int32, (1, 2 * span), 1)
+    side = column // span
+    within = column % span
+    col_pos = (
+        (within // half_block) % blocks * (2 * half_block) + side * half_block + within % half_block
+    )
+    same_old = within // (blocks * half_block) == row_req
+    new_col = lax.broadcasted_iota(jnp.int32, (1, local), 1)
+    new_mask = (new_col % each == row_req) & (new_col // each <= row_step)
+    scaling = 1.0 / math.sqrt(head)
+    contract = (((1,), (1,)), ((), ()))
+
+    for group in range(req // each):
+        limit = jnp.concatenate([length[group * each : (group + 1) * each]] * steps, axis=0)
+        bias[group] = jnp.where(same_old & (col_pos < limit), 0.0, neg_fill)
+    new_bias[...] = jnp.where(new_mask, 0.0, neg_fill)
 
     arrive(here + other_x, 0)
     arrive(here + other_x, 1)
@@ -433,22 +502,22 @@
     low_y = low_part(z, hidden_y[...], adapters_y)
     low[0] = low_part(z, hidden_v[:, mine], adapters)
     pages_copy.wait_recv()
-    for source in (1, 2):
-        arrive(far[source] * 2 + other_x, 0)
-        arrive(far[source] * 2 + other_x, 1)
-        low_y = low_y + low_part(far[source], hidden_y[...], adapters_y)
-        low[0] = low[0] + low_part(far[source], hidden_v[:, mine], adapters)
+    for source in (far[1], first_z):
+        arrive(source * 2 + other_x, 0)
+        arrive(source * 2 + other_x, 1)
+        low_y = low_y + low_part(source, hidden_y[...], adapters_y)
+        low[0] = low[0] + low_part(source, hidden_v[:, mine], adapters)
     arrive(last + other_x, 0)
     up_copy = pair(ups.at[t], ups.at[t], 3)
     arrive(last + other_x, 1)
-    low_y = spread(low_y + low_part(far[3], hidden_y[...], adapters_y))
+    low_y = spread(low_y + low_part(second_z, hidden_y[...], adapters_y))
     joined = low_y[:req]
     for s in range(1, steps):
         joined = jnp.where(lane_group == s, low_y[s * req : (s + 1) * req], joined)
     packed_low[0] = joined
     remote(packed_low.at[0], packed_low.at[1], cross_send.at[2], cross_recv.at[2], y_dev)
     remote(packed_low.at[0], packed_low.at[2], cross_send.at[3], cross_recv.at[3], yt_dev)
-    low[0] = low[0] + low_part(far[3], hidden_v[:, mine], adapters)
+    low[0] = low[0] + low_part(second_z, hidden_v[:, mine], adapters)
     low_copy = pair(low.at[0], low.at[1], 2)
     up_copy.wait_recv()
 
@@ -479,24 +548,6 @@
     fresh_q[...] = rounded(rotated(base[0, :, :head] + base[1, :, :head] + term[:, :head]))
     fresh_v[...] = base[0, :, 2 * head :] + base[1, :, 2 * head :] + term[:, head:]
 
-    each = 8
-    local = steps * each
-    span = each * blocks * half_block
-    down_row = lax.broadcasted_iota(jnp.int32, (local, 1), 0)
-    row_req = down_row % each
-    row_step = down_row // each
-    column = lax.broadcasted_iota(jnp.int32, (1, 2 * span), 1)
-    side = column // span
-    inner = column % span
-    col_pos = (
-        (inner // half_block) % blocks * (2 * half_block) + side * half_block + inner % half_block
-    )
-    same_old = inner // (blocks * half_block) == row_req
-    new_col = lax.broadcasted_iota(jnp.int32, (1, local), 1)
-    new_mask = (new_col % each == row_req) & (new_col // each <= row_step)
-    scaling = 1.0 / math.sqrt(head)
-    contract = (((1,), (1,)), ((), ()))
-
     for group in range(req // each):
         def picked(ref):
             return jnp.concatenate(
@@ -504,23 +555,21 @@
                 axis=0,
             ).astype(jnp.bfloat16)
 
-        limit = jnp.concatenate([length[group * each : (group + 1) * each]] * steps, axis=0)
         cached = jnp.concatenate(
             [pages[h, group * span : (group + 1) * span, :] for h in range(2)], axis=0
         )
         query, key, value = picked(fresh_q), picked(fresh_k), picked(fresh_v)
-        old_mask = same_old & (col_pos < limit)
         old = lax.dot_general(
             query, cached[:, :head], contract, preferred_element_type=jnp.float32
         )
         new = lax.dot_general(query, key, contract, preferred_element_type=jnp.float32)
-        old = jnp.where(old_mask, old * scaling, neg_fill)
-        new = jnp.where(new_mask, new * scaling, neg_fill)
+        old = old * scaling + bias[group]
+        new = new * scaling + new_bias[...]
         peak = jnp.maximum(
             jnp.max(old, axis=1, keepdims=True), jnp.max(new, axis=1, keepdims=True)
         )
-        old = jnp.where(old_mask, jnp.exp(old - peak), 0.0)
-        new = jnp.where(new_mask, jnp.exp(new - peak), 0.0)
+        old = jnp.exp(old - peak)
+        new = jnp.exp(new - peak)
         total = jnp.sum(old, axis=1, keepdims=True) + jnp.sum(new, axis=1, keepdims=True)
         mixed = jnp.dot(
             old.astype(jnp.bfloat16), cached[:, head:], preferred_element_type=jnp.float32
@@ -531,6 +580,12 @@
 
     for copy in sent:
         copy.wait_send()
+
+    @pl.when(inner)
+    def _():
+        for copies in relays:
+            for copy in copies:
+                copy.wait_send()
 
 
 def adapters_to_rows(
@@ -576,6 +631,8 @@
             pltpu.VMEM((rows, width // 2), hidden.dtype),
             pltpu.VMEM((2, 1, req), jnp.int32),
             pltpu.VMEM((3, req, 8 * rank), jnp.float32),
+            pltpu.VMEM((req // 8, 8 * steps, entries // req * half_block * 16), jnp.float32),
+            pltpu.VMEM((8 * steps, 8 * steps), jnp.float32),
             pltpu.VMEM((rows, head), jnp.float32),
             pltpu.VMEM((rows, head), jnp.float32),
             pltpu.VMEM((rows, head), jnp.float32),
@@ -590,6 +647,8 @@
             pltpu.SemaphoreType.DMA((4,)),
             pltpu.SemaphoreType.DMA((4,)),
             pltpu.SemaphoreType.DMA((4,)),
+            pltpu.SemaphoreType.DMA((8,)),
+            pltpu.SemaphoreType.DMA((8,)),
         ],
         compiler_params=pltpu.CompilerParams(
             collective_id=0, has_side_effects=True, vmem_limit_bytes=64 * 1024 * 1024

time: 32.2 us -> 30.7 us (0.953)
  Pallas kernels: 30.2 us -> 28.7 us
    pallas_call x1, Pallas kernels: 30.2 us -> 28.7 us  [adapters_to_rows(): pl.pallas_call(functools.partial(gather_kernel, steps), out_shape=jax.Sha...]
where the time goes in v4:
time: 30.7 us; the launch traced here: 30.3 us
  Pallas kernels  28.7 us (93%)
  other arithmetic  1.54 us (5%)
    pallas_call x1, Pallas kernels, adapters_to_rows(): pl.pallas_call(functools.partial(gather_kernel, steps), out_shape=jax.Sha...  28.7 us
    convert_element_type x1, other arithmetic, adapters_to_rows(): return result.astype(jnp.bfloat16)  1.54 us

profile of v4, /device:TPU:1, one launch (start us, length us, event | category | flops | bytes accessed | tf_op | source)
XLA Modules:
  0.0 30.3 jit_solution(17318197893414086858)
XLA Ops:
  0.0 28.7 %shard_map.91 = f32[4,64,128]{2,1,0:T(8,128)} custom-call(bf16[256,2048]{1,0:T(8,128)(2,1)} %bitcast.5, bf16[2048,384]{1,0:T(8,128)(2,1)} %weight_hbm.1, bf16[2,32,2048]{2,1,0:T(8,128)(2,1)} %bitcast.7, bf16[2,16,256]{2,1,0:T(8,128)(2,1)} %up_hbm.1, bf16[192,8,256]{2,1,0:T(8,128)(2,1)} %bitcast.6, s32[1,64]{1,0:T(1,128)} %bitcast.8, s32[1,64]{1,0:T(1,128)} %bitcast.9, ...), custom_call_target="tpu_custom_call" | custom-call | tf_op jit(solution)/shard_map/pallas_call | solution.py:611
  28.8 1.5 %convert_element_type.3 = bf16[4,64,128]{2,1,0:T(8,128)(2,1)} convert(f32[4,64,128]{2,1,0:T(8,128)} %shard_map.91) | non-fusion elementwise | flops 32768 | bytes 196608 | tf_op jit(solution)/shard_map/convert_element_type | solution.py:667

commit v5 on v4

--- a/solution.py
+++ b/solution.py
@@ -548,33 +548,50 @@
     fresh_q[...] = rounded(rotated(base[0, :, :head] + base[1, :, :head] + term[:, :head]))
     fresh_v[...] = base[0, :, 2 * head :] + base[1, :, 2 * head :] + term[:, head:]
 
-    for group in range(req // each):
-        def picked(ref):
-            return jnp.concatenate(
-                [ref[s * req + group * each : s * req + (group + 1) * each, :] for s in range(steps)],
-                axis=0,
-            ).astype(jnp.bfloat16)
-
-        cached = jnp.concatenate(
-            [pages[h, group * span : (group + 1) * span, :] for h in range(2)], axis=0
+    def picked(ref, group):
+        return jnp.concatenate(
+            [ref[s * req + group * each : s * req + (group + 1) * each, :] for s in range(steps)],
+            axis=0,
+        ).astype(jnp.bfloat16)
+
+    groups = range(req // each)
+    spans = [slice(group * span, (group + 1) * span) for group in groups]
+    queries = [picked(fresh_q, group) for group in groups]
+    olds, news, totals = [], [], []
+    for group in groups:
+        keys = jnp.concatenate([pages[h, spans[group], :head] for h in range(2)], axis=0)
+        old = lax.dot_general(queries[group], keys, contract, preferred_element_type=jnp.float32)
+        new = lax.dot_general(
+            queries[group],
+            picked(fresh_k, group),
+            contract,
+            preferred_element_type=jnp.float32,
         )
-        query, key, value = picked(fresh_q), picked(fresh_k), picked(fresh_v)
-        old = lax.dot_general(
-            query, cached[:, :head], contract, preferred_element_type=jnp.float32
+        olds.append(old * scaling + bias[group])
+        news.append(new * scaling + new_bias[...])
+    peaks = [
+        jnp.maximum(jnp.max(old, axis=1, keepdims=True), jnp.max(new, axis=1, keepdims=True))
+        for old, new in zip(olds, news)
+    ]
+    olds = [jnp.exp(old - peak) for old, peak in zip(olds, peaks)]
+    news = [jnp.exp(new - peak) for new, peak in zip(news, peaks)]
+    totals = [
+        jnp.sum(old, axis=1, keepdims=True) + jnp.sum(new, axis=1, keepdims=True)
+        for old, new in zip(olds, news)
+    ]
+    mixes = []
+    for group in groups:
+        values = jnp.concatenate([pages[h, spans[group], head:] for h in range(2)], axis=0)
+        mixes.append(
+            jnp.dot(olds[group].astype(jnp.bfloat16), values, preferred_element_type=jnp.float32)
+            + jnp.dot(
+                news[group].astype(jnp.bfloat16),
+                picked(fresh_v, group),
+                preferred_element_type=jnp.float32,
+            )
         )
-        new = lax.dot_general(query, key, contract, preferred_element_type=jnp.float32)
-        old = old * scaling + bias[group]
-        new = new * scaling + new_bias[...]
-        peak = jnp.maximum(
-            jnp.max(old, axis=1, keepdims=True), jnp.max(new, axis=1, keepdims=True)
-        )
-        old = jnp.exp(old - peak)
-        new = jnp.exp(new - peak)
-        total = jnp.sum(old, axis=1, keepdims=True) + jnp.sum(new, axis=1, keepdims=True)
-        mixed = jnp.dot(
-            old.astype(jnp.bfloat16), cached[:, head:], preferred_element_type=jnp.float32
-        ) + jnp.dot(new.astype(jnp.bfloat16), value, preferred_element_type=jnp.float32)
-        mixed = mixed / total
+    for group in groups:
+        mixed = mixes[group] / totals[group]
         for s in range(steps):
             out_ref[s, group * each : (group + 1) * each, :] = mixed[s * each : (s + 1) * each]
 

time: 30.7 us -> 29.1 us (0.948)
  Pallas kernels: 28.7 us -> 27.1 us
    pallas_call x1, Pallas kernels: 28.7 us -> 27.1 us  [adapters_to_rows(): pl.pallas_call(functools.partial(gather_kernel, steps), out_shape=jax.Sha...]
where the time goes in v5:
time: 29.1 us; the launch traced here: 28.7 us
  Pallas kernels  27.1 us (93%)
  other arithmetic  1.54 us (5%)
    pallas_call x1, Pallas kernels, adapters_to_rows(): pl.pallas_call(functools.partial(gather_kernel, steps), out_shape=jax.Sha...  27.1 us
    convert_element_type x1, other arithmetic, adapters_to_rows(): return result.astype(jnp.bfloat16)  1.54 us

profile of v5, /device:TPU:1, one launch (start us, length us, event | category | flops | bytes accessed | tf_op | source)
XLA Modules:
  0.0 28.7 jit_solution(10914032395517007946)
XLA Ops:
  0.0 27.1 %shard_map.91 = f32[4,64,128]{2,1,0:T(8,128)} custom-call(bf16[256,2048]{1,0:T(8,128)(2,1)} %bitcast.5, bf16[2048,384]{1,0:T(8,128)(2,1)} %weight_hbm.1, bf16[2,32,2048]{2,1,0:T(8,128)(2,1)} %bitcast.7, bf16[2,16,256]{2,1,0:T(8,128)(2,1)} %up_hbm.1, bf16[192,8,256]{2,1,0:T(8,128)(2,1)} %bitcast.6, s32[1,64]{1,0:T(1,128)} %bitcast.8, s32[1,64]{1,0:T(1,128)} %bitcast.9, ...), custom_call_target="tpu_custom_call" | custom-call | tf_op jit(solution)/shard_map/pallas_call | solution.py:628
  27.1 1.5 %convert_element_type.3 = bf16[4,64,128]{2,1,0:T(8,128)(2,1)} convert(f32[4,64,128]{2,1,0:T(8,128)} %shard_map.91) | non-fusion elementwise | flops 32768 | bytes 196608 | tf_op jit(solution)/shard_map/convert_element_type | solution.py:684
